TPU v7x, 32 devices: a whole 2x2x4 slice. The times are simulated.
32 devices in a mesh: dp: 2 (over core), head: 4 (over y, x), mlp: 4 (over z).
Axes of the slice: x: 2, y: 2, z: 4, core: 2. Of those that a mesh axis runs over, the one named last changes fastest.
Arguments:
- tokens: bfloat16 [2048, 8, 1024], P('head', ('dp', 'mlp')), may hold values from -6 to 6
- first_values: bfloat16 [2048, 8, 1024], P(None, ('dp', 'mlp'), 'head'), may hold values from -10.5 to 10.5
- segment_ids: int32 [2048, 8], P(None, ('dp', 'mlp')), may hold values from 0 to 7, as said below
- positions: int32 [2048, 8], P(None, ('dp', 'mlp')), may hold values from 0 to 2047, as said below
- attn_gain: float32 [1024], replicated, may hold values from 0.5 to 1.5
- w_query: bfloat16 [1024, 1024], P(None, 'head'), may hold values from -0.1875 to 0.1875
- w_key: bfloat16 [1024, 1024], P(None, 'head'), may hold values from -0.1875 to 0.1875
- w_value: bfloat16 [1024, 1024], P(None, 'head'), may hold values from -0.1875 to 0.1875
- w_out: bfloat16 [1024, 1024], P('head'), may hold values from -2 to 2
- mlp_gain: float32 [1024], replicated, may hold values from 0.5 to 1.5
- w_gate: bfloat16 [1024, 2816], P(None, 'mlp'), may hold values from -0.1875 to 0.1875
- w_up: bfloat16 [1024, 2816], P(None, 'mlp'), may hold values from -0.1875 to 0.1875
- w_down: bfloat16 [2816, 1024], P('mlp'), may hold values from -0.109375 to 0.109375
- out_grad: bfloat16 [2048, 8, 1024], P('head', ('dp', 'mlp')), may hold values from -6 to 6
Outputs:
- output: bfloat16 [2048, 8, 1024], P('head', ('dp', 'mlp'))
- input_grad: bfloat16 [2048, 8, 1024], P('head', ('dp', 'mlp'))
- first_values_grad: bfloat16 [2048, 8, 1024], P(None, ('dp', 'mlp'), 'head')
- attn_gain_grad: float32 [1024], replicated
- w_query_grad: float32 [1024, 1024], P(None, 'head')
- w_key_grad: float32 [1024, 1024], P(None, 'head')
- w_value_grad: float32 [1024, 1024], P(None, 'head')
- w_out_grad: float32 [1024, 1024], P('head')
- mlp_gain_grad: float32 [1024], replicated
- w_gate_grad: float32 [1024, 2816], P(None, 'mlp')
- w_up_grad: float32 [1024, 2816], P(None, 'mlp')
- w_down_grad: float32 [2816, 1024], P('mlp')
- value_norms: float32 [2], replicated
Inputs may be any that keep to these rules, and one draw needn't show every extreme that they name: `segment_ids`: along each packed row (dimension 0) the ids start at 0 and rise by at most one from one position to the next; packed row 0 holds a single document, every other packed row exactly 8. `positions`: 0 at a row's start and wherever the segment id changes, else one more than at the previous position.
All inputs are finite; a program needn't handle non-finite values.
Results may differ from a plain program's by a relative error of at most 0.019.
Values may be sent and summed in bfloat16 or wider, within the bound.
No kernel may reach another device: no remote copies, remote signals or barrier semaphores. Data moves between devices by JAX's collectives and lax.ppermute only.
A program may use at most 256 MiB of HBM per device.

v0:
```python
import jax
import jax.numpy as jnp
from jax import lax
from jax.sharding import PartitionSpec as P

HEAD_DIM = 64
epsilon = 1e-06
theta_base = 10000.0
blend_weight = 0.5
masked_score = -1e30


def rms_scale(rows):
    return lax.rsqrt(jnp.mean(rows * rows, axis=-1, keepdims=True) + epsilon)


def norm_back(rows, scale, gain, grad):
    weighted = grad * gain
    row_grad = scale * weighted - rows * scale * scale * scale * jnp.mean(
        weighted * rows, axis=-1, keepdims=True
    )
    gain_grad = jnp.sum(grad * rows * scale, axis=(0, 1))
    return (row_grad, gain_grad)


def rotate(values, places, direction):
    half = values.shape[-1] // 2
    freq = theta_base ** (-jnp.arange(half, dtype=jnp.float32) * 2.0 / values.shape[-1])
    angles = places.astype(jnp.float32)[..., None] * freq
    cosine = jnp.cos(angles)[:, :, None, :]
    sine = direction * jnp.sin(angles)[:, :, None, :]
    first, second = (values[..., :half], values[..., half:])
    return jnp.concatenate(
        [first * cosine - second * sine, second * cosine + first * sine], axis=-1
    )


def by_rows(array, heads):
    return jnp.moveaxis(array.reshape(array.shape[0], array.shape[1], heads, -1), 1, 0)


def block_scores(queries, keys, segments, number, block):
    length = keys.shape[0]
    begin = number * block
    query_block = lax.dynamic_slice_in_dim(queries, begin, block, 0)
    query_index = begin + jnp.arange(block, dtype=jnp.int32)
    key_index = jnp.arange(length, dtype=jnp.int32)
    query_segments = lax.dynamic_slice_in_dim(segments, begin, block, 0)
    allowed = (key_index[None, :] <= query_index[:, None]) & (
        segments[None, :] == query_segments[:, None]
    )
    scores = jnp.einsum(
        "qhd,khd->hqk", query_block, keys, preferred_element_type=jnp.float32
    ) * HEAD_DIM ** (-0.5)
    return (query_block, jnp.where(allowed[None], scores, masked_score))


def attend_forward(queries, keys, values, segments, block):
    length = queries.shape[0]

    def one_block(carry, number):
        query_block, scores = block_scores(queries, keys, segments, number, block)
        top = jnp.max(scores, axis=-1, keepdims=True)
        log_total = top + jnp.log(jnp.sum(jnp.exp(scores - top), axis=-1, keepdims=True))
        weights = jnp.exp(scores - log_total).astype(jnp.bfloat16)
        mixed = jnp.einsum("hqk,khd->qhd", weights, values, preferred_element_type=jnp.float32)
        return (carry, (mixed, log_total))

    _, (mixed, log_total) = lax.scan(one_block, 0, jnp.arange(length // block))
    return (mixed.reshape(length, mixed.shape[2], mixed.shape[3]), log_total)


def attend_backward(queries, keys, values, segments, mixed_grad, log_total, block):
    length = queries.shape[0]
    scale = HEAD_DIM ** (-0.5)

    def one_block(carry, number):
        key_grad, value_grad = carry
        query_block, scores = block_scores(queries, keys, segments, number, block)
        probs = jnp.exp(scores - log_total[number])
        weights = probs.astype(jnp.bfloat16)
        grad_block = lax.dynamic_slice_in_dim(mixed_grad, number * block, block, 0)
        weight_grad = jnp.einsum(
            "qhd,khd->hqk", grad_block, values, preferred_element_type=jnp.float32
        )
        score_grad = (
            probs * (weight_grad - jnp.sum(probs * weight_grad, axis=-1, keepdims=True))
        ).astype(jnp.bfloat16)
        query_grad = (
            jnp.einsum("hqk,khd->qhd", score_grad, keys, preferred_element_type=jnp.float32) * scale
        )
        key_grad = (
            key_grad
            + jnp.einsum(
                "hqk,qhd->khd", score_grad, query_block, preferred_element_type=jnp.float32
            )
            * scale
        )
        value_grad = value_grad + jnp.einsum(
            "hqk,qhd->khd", weights, grad_block, preferred_element_type=jnp.float32
        )
        return ((key_grad, value_grad), query_grad)

    zeros = jnp.zeros(keys.shape, jnp.float32)
    (key_grad, value_grad), query_grad = lax.scan(
        one_block, (zeros, zeros), jnp.arange(length // block)
    )
    return (query_grad.reshape(keys.shape), key_grad, value_grad)


def on_device(
    tokens,
    first_values,
    segment_ids,
    positions,
    attn_gain,
    w_query,
    w_key,
    w_value,
    w_out,
    mlp_gain,
    w_gate,
    w_up,
    w_down,
    out_grad,
):
    width = w_query.shape[1]
    heads_here = width // HEAD_DIM
    length = segment_ids.shape[0]
    rows_here = tokens.shape[1]
    block = min(512, length)
    ff_here = w_gate.shape[1]
    residual = tokens.astype(jnp.float32)
    attn_scale = rms_scale(residual)
    attn_input = (residual * attn_scale * attn_gain).astype(jnp.bfloat16)
    w_project = jnp.concatenate([w_query, w_key, w_value], axis=1)
    piece = lax.all_gather(attn_input, "head", axis=0, tiled=True)
    count = piece.shape[0]
    joined = jnp.einsum("lrd,dh->lrh", piece, w_project, preferred_element_type=jnp.float32)
    query_part = joined[..., :width].reshape(count, rows_here, heads_here, HEAD_DIM)
    key_part = joined[..., width : 2 * width].reshape(count, rows_here, heads_here, HEAD_DIM)
    queries = (
        rotate(query_part, positions, 1.0).reshape(count, rows_here, width).astype(jnp.bfloat16)
    )
    keys = rotate(key_part, positions, 1.0).reshape(count, rows_here, width).astype(jnp.bfloat16)
    gathered, queries, keys, value_proj = (piece, queries, keys, joined[..., 2 * width :])
    firsts = first_values.astype(jnp.float32)
    blended = blend_weight * value_proj + (1.0 - blend_weight) * firsts
    blended_low = blended.astype(jnp.bfloat16)
    first_heads = firsts.reshape(length, rows_here, heads_here, HEAD_DIM)
    blend_heads = blended.reshape(length, rows_here, heads_here, HEAD_DIM)
    norm_local = jnp.stack(
        [
            jnp.sum(jnp.sqrt(jnp.sum(first_heads * first_heads, axis=-1))),
            jnp.sum(jnp.sqrt(jnp.sum(blend_heads * blend_heads, axis=-1))),
        ]
    )
    segment_rows = jnp.transpose(segment_ids, (1, 0))
    query_rows = by_rows(queries, heads_here)
    key_rows = by_rows(keys, heads_here)
    value_rows = by_rows(blended_low, heads_here)

    def forward_row(item):
        return attend_forward(item[0], item[1], item[2], item[3], block)

    mixed, log_total = lax.map(forward_row, (query_rows, key_rows, value_rows, segment_rows))
    attn_mixed = jnp.moveaxis(mixed, 0, 1).reshape(length, rows_here, width).astype(jnp.bfloat16)
    part = attn_mixed
    attn_branch = lax.psum_scatter(
        jnp.einsum("lrh,hd->lrd", part, w_out, preferred_element_type=jnp.float32),
        "head",
        scatter_dimension=0,
        tiled=True,
    )
    hidden_state = residual + attn_branch
    mlp_scale = rms_scale(hidden_state)
    mlp_input = (hidden_state * mlp_scale * mlp_gain).astype(jnp.bfloat16)
    w_gate_up = jnp.concatenate([w_gate, w_up], axis=1)
    piece = lax.all_gather(mlp_input, "mlp", axis=1, tiled=True)
    joined = jnp.einsum("lrd,df->lrf", piece, w_gate_up, preferred_element_type=jnp.float32)
    gate = joined[..., :ff_here]
    up = joined[..., ff_here:]
    expand_hidden = (jax.nn.silu(gate) * up).astype(jnp.bfloat16)
    mlp_gathered = piece
    down_terms = jnp.einsum(
        "lrf,fd->lrd", expand_hidden, w_down, preferred_element_type=jnp.float32
    )
    mlp_branch = lax.psum_scatter(
        down_terms.astype(jnp.bfloat16), "mlp", scatter_dimension=1, tiled=True
    ).astype(jnp.float32)
    output = (hidden_state + mlp_branch).astype(jnp.bfloat16)
    piece = lax.all_gather(out_grad, "mlp", axis=1, tiled=True)
    down_sum = jnp.einsum("lrf,lrd->fd", expand_hidden, piece, preferred_element_type=jnp.float32)
    part_grad = jnp.einsum("lrd,fd->lrf", piece, w_down, preferred_element_type=jnp.float32)
    hidden_grad = part_grad
    gate, up = (gate, up)
    sigma = jax.nn.sigmoid(gate)
    gate_grad = (hidden_grad * up * sigma * (1.0 + gate * (1.0 - sigma))).astype(jnp.bfloat16)
    up_grad = (hidden_grad * gate * sigma).astype(jnp.bfloat16)
    gate_up_grad = jnp.concatenate([gate_grad, up_grad], axis=-1)
    gate_up_wgrad = jnp.einsum(
        "lrd,lrf->df", mlp_gathered, gate_up_grad, preferred_element_type=jnp.float32
    )
    input_terms = jnp.einsum(
        "lrf,df->lrd", gate_up_grad, w_gate_up, preferred_element_type=jnp.float32
    )
    mlp_normed_grad = lax.psum_scatter(
        input_terms.astype(jnp.bfloat16), "mlp", scatter_dimension=1, tiled=True
    ).astype(jnp.float32)
    state_norm_grad, mlp_gain_grad = norm_back(hidden_state, mlp_scale, mlp_gain, mlp_normed_grad)
    state_grad = out_grad.astype(jnp.float32) + state_norm_grad
    state_grad_low = state_grad.astype(jnp.bfloat16)
    piece = lax.all_gather(state_grad_low, "head", axis=0, tiled=True)
    out_sum = jnp.einsum("lrh,lrd->hd", attn_mixed, piece, preferred_element_type=jnp.float32)
    part_grad = jnp.einsum("lrd,hd->lrh", piece, w_out, preferred_element_type=jnp.float32)
    out_wgrad = out_sum
    mixed_grad_low = part_grad.astype(jnp.bfloat16)
    mixed_grad_rows = by_rows(mixed_grad_low, heads_here)

    def backward_row(item):
        return attend_backward(item[0], item[1], item[2], item[3], item[4], item[5], block)

    query_grad, key_grad, blend_grad = lax.map(
        backward_row, (query_rows, key_rows, value_rows, segment_rows, mixed_grad_rows, log_total)
    )
    query_grad = jnp.moveaxis(query_grad, 0, 1)
    key_grad = jnp.moveaxis(key_grad, 0, 1)
    blend_low = (
        jnp.moveaxis(blend_grad, 0, 1).reshape(length, rows_here, width).astype(jnp.bfloat16)
    )
    query_pre = (
        rotate(query_grad, positions, -1.0).reshape(length, rows_here, width).astype(jnp.bfloat16)
    )
    key_pre = (
        rotate(key_grad, positions, -1.0).reshape(length, rows_here, width).astype(jnp.bfloat16)
    )
    value_pre = (blend_weight * blend_low.astype(jnp.float32)).astype(jnp.bfloat16)
    first_values_grad = ((1.0 - blend_weight) * blend_low.astype(jnp.float32)).astype(jnp.bfloat16)
    proj_grad = jnp.concatenate([query_pre, key_pre, value_pre], axis=-1)
    proj_wgrad = jnp.einsum("lrd,lrh->dh", gathered, proj_grad, preferred_element_type=jnp.float32)
    part = proj_grad
    attn_normed_grad = lax.psum_scatter(
        jnp.einsum("lrh,dh->lrd", part, w_project, preferred_element_type=jnp.float32).astype(
            jnp.bfloat16
        ),
        "head",
        scatter_dimension=0,
        tiled=True,
    ).astype(jnp.float32)
    input_norm_grad, attn_gain_grad = norm_back(residual, attn_scale, attn_gain, attn_normed_grad)
    input_grad = (state_grad + input_norm_grad).astype(jnp.bfloat16)
    query_wgrad, key_wgrad, value_wgrad, out_wgrad = (
        lax.psum(proj_wgrad[:, :width].astype(jnp.bfloat16), ("dp", "mlp")).astype(jnp.float32),
        lax.psum(proj_wgrad[:, width : 2 * width].astype(jnp.bfloat16), ("dp", "mlp")).astype(
            jnp.float32
        ),
        lax.psum(proj_wgrad[:, 2 * width :].astype(jnp.bfloat16), ("dp", "mlp")).astype(
            jnp.float32
        ),
        lax.psum(out_wgrad.astype(jnp.bfloat16), ("dp", "mlp")).astype(jnp.float32),
    )
    gate_wgrad, up_wgrad, down_wgrad = (
        lax.psum(gate_up_wgrad[:, :ff_here].astype(jnp.bfloat16), ("dp", "head")).astype(
            jnp.float32
        ),
        lax.psum(gate_up_wgrad[:, ff_here:].astype(jnp.bfloat16), ("dp", "head")).astype(
            jnp.float32
        ),
        lax.psum(down_sum.astype(jnp.bfloat16), ("dp", "head")).astype(jnp.float32),
    )
    attn_gain_total, mlp_gain_total, norm_total = lax.psum(
        (attn_gain_grad, mlp_gain_grad, norm_local), ("dp", "head", "mlp")
    )
    count_all = (
        length
        * rows_here
        * heads_here
        * lax.axis_size("dp")
        * lax.axis_size("head")
        * lax.axis_size("mlp")
    )
    value_norms = norm_total / count_all
    return (
        output,
        input_grad,
        first_values_grad,
        attn_gain_total,
        query_wgrad,
        key_wgrad,
        value_wgrad,
        out_wgrad,
        mlp_gain_total,
        gate_wgrad,
        up_wgrad,
        down_wgrad,
        value_norms,
    )


def solution(mesh):
    placed = (
        P("head", ("dp", "mlp"), None),
        P(None, ("dp", "mlp"), "head"),
        P(None, ("dp", "mlp")),
        P(None, ("dp", "mlp")),
        P(),
        P(None, "head"),
        P(None, "head"),
        P(None, "head"),
        P("head", None),
        P(),
        P(None, "mlp"),
        P(None, "mlp"),
        P("mlp", None),
        P("head", ("dp", "mlp"), None),
    )
    return jax.shard_map(
        on_device,
        mesh=mesh,
        in_specs=placed,
        out_specs=(
            P("head", ("dp", "mlp"), None),
            P("head", ("dp", "mlp"), None),
            P(None, ("dp", "mlp"), "head"),
            P(),
            P(None, "head"),
            P(None, "head"),
            P(None, "head"),
            P("head", None),
            P(),
            P(None, "mlp"),
            P(None, "mlp"),
            P("mlp", None),
            P(),
        ),
        check_vma=False,
    )
```

profile of v0, /device:TPU:0, one launch (start us, length us, event | category | flops | bytes accessed | tf_op | source)
XLA Modules:
  0.0 1060.9 jit_solution(17914866796289467341)
XLA Ops:
  19.0 48.6 %all-gather.5.cloned.1.call-done = bf16[2048,1,1024]{2,0,1:T(8,128)(2,1)} async-done(((bf16[512,1,1024]{2,0,1:T(8,128)(2,1)}), bf16[2048,1,1024]{2,0,1:T(8,128)(2,1)}) %all-gather.5.cloned.1.call-update) | async-done | bytes 4194320 | tf_op jit(solution)/shard_map/all_gather | solution.py:137
  67.6 5.8 fusion.45
  78.5 68.2 %while.47 = (s32[]{:T(128)}, bf16[4,512,4,64]{1,3,2,0:T(8,128)(2,1)}, f32[4,4,512,1]{2,1,3,0:T(4,128)}, s32[4]{0:T(128)S(1)}, s32[2048]{0:T(1024)S(1)}, /*index=...) while((s32[]{:T(128)}, ...), condition=%wide.region_4.0_spmd, body=%wide.region_1.4_spmd.sunk | while | flops 1123023360 | bytes 65882372 | solution.py:69
  89.2 5.5 fusion.136
  106.2 5.5 fusion.136
  123.2 5.5 fusion.136
  140.2 5.5 fusion.136
  150.4 4.6 convolution_bitcast_fusion
  155.0 86.5 %reduce-scatter.5.cloned.1.call-done = f32[512,1,1024]{2,0,1:T(8,128)} async-done(((f32[2048,1,1024]{2,0,1:T(8,128)}), f32[512,1,1024]{2,0,1:T(8,128)}) %reduce-scatter.5.cloned.1.call-update) | async-done | bytes 2097168 | tf_op jit(solution)/shard_map/reduce_scatter | solution.py:169
  253.5 75.0 %all-gather.7.cloned.1.call-done = bf16[512,4,1024]{2,0,1:T(8,128)(2,1)} async-done(((bf16[512,1,1024]{2,0,1:T(8,128)(2,1)}), bf16[512,4,1024]{2,0,1:T(8,128)(2,1)}) %all-gather.7.cloned.1.call-update) | async-done | bytes 4194320 | tf_op jit(solution)/shard_map/all_gather | solution.py:179
  328.5 13.2 %fusion.74 = f32[512,4,1408]{0,2,1:T(8,128)} fusion(bf16[512,4,1024]{2,0,1:T(8,128)(2,1)} %all-gather.7.cloned.1.call-done, bf16[1024,704]{1,0:T(8,128)(2,1)} %copy.69, bf16[1024,704]{1,0:T(8,128)(2,1)} %copy.68), kind=kOutput, calls=%fused_computation.106 | convolution fusion | flops 5911347200 | bytes 18612224 | tf_op jit(solution)/shard_map/lrd,df->lrf/dot_general | solution.py:180
  341.7 67.6 %all-gather.9.cloned.1.call-done = bf16[512,4,1024]{2,0,1:T(8,128)(2,1)} async-done(((bf16[512,1,1024]{2,0,1:T(8,128)(2,1)}), bf16[512,4,1024]{2,0,1:T(8,128)(2,1)}) %all-gather.9.cloned.1.call-update) | async-done | bytes 4194320 | tf_op jit(solution)/shard_map/all_gather | solution.py:192
  409.3 10.6 multiply_convert_fusion.2
  422.4 9.5 fusion.49
  432.4 75.0 %reduce-scatter.9.cloned.1.call-done = bf16[512,1,1024]{2,0,1:T(8,128)(2,1)} async-done(((bf16[512,4,1024]{2,0,1:T(8,128)(2,1)}), bf16[512,1,1024]{2,0,1:T(8,128)(2,1)}) %reduce-scatter.9.cloned.1.call-update) | async-done | bytes 1048592 | tf_op jit(solution)/shard_map/reduce_scatter | solution.py:207
  514.7 10.4 bitcast_convert_fusion
  532.8 35.1 %all-gather.11.cloned.1.call-done = bf16[2048,1,1024]{2,0,1:T(8,128)(2,1)} async-done(((bf16[512,1,1024]{2,0,1:T(8,128)(2,1)}), bf16[2048,1,1024]{2,0,1:T(8,128)(2,1)}) %all-gather.11.cloned.1.call-update) | async-done | bytes 4194320 | tf_op jit(solution)/shard_map/all_gather | solution.py:213
  568.0 4.4 fusion.50
  572.4 260.4 %while.48 = (s32[]{:T(128)}, f32[2048,4,64]{0,2,1:T(8,128)}, f32[2048,4,64]{0,2,1:T(8,128)}, f32[4,512,4,64]{1,0,3,2:T(4,128)}, s32[4]{0:T(128)S(1)}, /*index=5*...) while((s32[]{:T(128)}, f32[2048,4,64]{0,2,1:T(8,128)}, ...), condition=%wide.region_12.13_spmd.clone, body=%wide.region_10.12_spmd.clone.sunk | while | flops 2753165824 | bytes 212412720 | solution.py:105
  580.6 5.8 copy-done.1
  586.5 7.2 fusion.149
  593.6 13.0 %multiply_reduce_fusion.3 = (f32[4,512]{1,0:T(4,128)S(1)}, f32[4,512,2048]{2,1,0:T(8,128)}) fusion(f32[4,512,2048]{2,1,0:T(8,128)} %copy-done.1, f32[4,512]{1,0:T(4,128)S(1)} %dynamic-slice_bitcast_fusion.2, pred[512,2048]{1,0:T(8,128)(4,1)S(1)} %fusion.147, bf16[2048,4,64]{0,2,1:T(8,128)(2,1)} %get-tuple-element.557, ...), kind=kOutput, calls=%fused_computation.19.clone.1 | convolution fusion | flops 557840384 | bytes 35930116 | tf_op jit(solution)/shard_map/while/body/eval_jaxpr/while/body/eval_jaxpr/qhd,khd->hqk/dot_general | solution.py:83
  606.6 12.3 %multiply_convert_fusion.7 = bf16[4,512,2048]{2,1,0:T(8,128)(2,1)S(1)} fusion(f32[4,512,2048]{2,1,0:T(8,128)} %get-tuple-element.477, f32[4,512,2048]{2,1,0:T(8,128)} %copy-done.1, f32[4,512]{1,0:T(4,128)S(1)} %get-tuple-element.478, f32[4,512]{1,0:T(4,128)S(1)} %dynamic-slice_bitcast_fusion.2, pred[512,2048]{1,0:T(8,128)(4,1)S(1)} %fusion.147), kind=kLoop, calls=%fused_computation.18.clone.1 | loop fusion | flops 25165824 | bytes 43008000 | tf_op jit(solution)/shard_map/while/body/eval_jaxpr/while/body/eval_jaxpr/convert_element_type | solution.py:88
  626.0 11.1 %dynamic_update_slice.31 = f32[4,512,4,64]{1,0,3,2:T(4,128)} dynamic-update-slice(f32[4,512,4,64]{1,0,3,2:T(4,128)} %get-tuple-element.534, f32[1,512,4,64]{1,0,3,2:T(1,128)S(1)} %copy.97, s32[]{:T(128)S(6)} %copy.116, s32[]{:T(128)} %constant.102.clone.1..sunk.1, s32[]{:T(128)} %constant.102.clone.1..sunk.1, s32[]{:T(128)} %constant.102.clone.1..sunk.1) | dynamic-update-slice | bytes 1048580 | tf_op jit(solution)/shard_map/while/body/eval_jaxpr/while/body/jit(dynamic_update_index_in_dim)/dynamic_update_slice | solution.py:69
  645.1 5.9 copy-done.1
  651.0 7.6 fusion.149
  658.6 12.8 %multiply_reduce_fusion.3 = (f32[4,512]{1,0:T(4,128)S(1)}, f32[4,512,2048]{2,1,0:T(8,128)}) fusion(f32[4,512,2048]{2,1,0:T(8,128)} %copy-done.1, f32[4,512]{1,0:T(4,128)S(1)} %dynamic-slice_bitcast_fusion.2, pred[512,2048]{1,0:T(8,128)(4,1)S(1)} %fusion.147, bf16[2048,4,64]{0,2,1:T(8,128)(2,1)} %get-tuple-element.557, ...), kind=kOutput, calls=%fused_computation.19.clone.1 | convolution fusion | flops 557840384 | bytes 35930116 | tf_op jit(solution)/shard_map/while/body/eval_jaxpr/while/body/eval_jaxpr/qhd,khd->hqk/dot_general | solution.py:83
  671.4 12.1 %multiply_convert_fusion.7 = bf16[4,512,2048]{2,1,0:T(8,128)(2,1)S(1)} fusion(f32[4,512,2048]{2,1,0:T(8,128)} %get-tuple-element.477, f32[4,512,2048]{2,1,0:T(8,128)} %copy-done.1, f32[4,512]{1,0:T(4,128)S(1)} %get-tuple-element.478, f32[4,512]{1,0:T(4,128)S(1)} %dynamic-slice_bitcast_fusion.2, pred[512,2048]{1,0:T(8,128)(4,1)S(1)} %fusion.147), kind=kLoop, calls=%fused_computation.18.clone.1 | loop fusion | flops 25165824 | bytes 43008000 | tf_op jit(solution)/shard_map/while/body/eval_jaxpr/while/body/eval_jaxpr/convert_element_type | solution.py:88
  686.1 4.7 fusion.148
  691.3 11.1 %dynamic_update_slice.31 = f32[4,512,4,64]{1,0,3,2:T(4,128)} dynamic-update-slice(f32[4,512,4,64]{1,0,3,2:T(4,128)} %get-tuple-element.534, f32[1,512,4,64]{1,0,3,2:T(1,128)S(1)} %copy.97, s32[]{:T(128)S(6)} %copy.116, s32[]{:T(128)} %constant.102.clone.1..sunk.1, s32[]{:T(128)} %constant.102.clone.1..sunk.1, s32[]{:T(128)} %constant.102.clone.1..sunk.1) | dynamic-update-slice | bytes 1048580 | tf_op jit(solution)/shard_map/while/body/eval_jaxpr/while/body/jit(dynamic_update_index_in_dim)/dynamic_update_slice | solution.py:69
  710.4 5.7 copy-done.1
  716.1 7.5 fusion.149
  723.7 12.8 %multiply_reduce_fusion.3 = (f32[4,512]{1,0:T(4,128)S(1)}, f32[4,512,2048]{2,1,0:T(8,128)}) fusion(f32[4,512,2048]{2,1,0:T(8,128)} %copy-done.1, f32[4,512]{1,0:T(4,128)S(1)} %dynamic-slice_bitcast_fusion.2, pred[512,2048]{1,0:T(8,128)(4,1)S(1)} %fusion.147, bf16[2048,4,64]{0,2,1:T(8,128)(2,1)} %get-tuple-element.557, ...), kind=kOutput, calls=%fused_computation.19.clone.1 | convolution fusion | flops 557840384 | bytes 35930116 | tf_op jit(solution)/shard_map/while/body/eval_jaxpr/while/body/eval_jaxpr/qhd,khd->hqk/dot_general | solution.py:83
  736.5 12.1 %multiply_convert_fusion.7 = bf16[4,512,2048]{2,1,0:T(8,128)(2,1)S(1)} fusion(f32[4,512,2048]{2,1,0:T(8,128)} %get-tuple-element.477, f32[4,512,2048]{2,1,0:T(8,128)} %copy-done.1, f32[4,512]{1,0:T(4,128)S(1)} %get-tuple-element.478, f32[4,512]{1,0:T(4,128)S(1)} %dynamic-slice_bitcast_fusion.2, pred[512,2048]{1,0:T(8,128)(4,1)S(1)} %fusion.147), kind=kLoop, calls=%fused_computation.18.clone.1 | loop fusion | flops 25165824 | bytes 43008000 | tf_op jit(solution)/shard_map/while/body/eval_jaxpr/while/body/eval_jaxpr/convert_element_type | solution.py:88
  751.2 4.7 fusion.148
  756.4 11.1 %dynamic_update_slice.31 = f32[4,512,4,64]{1,0,3,2:T(4,128)} dynamic-update-slice(f32[4,512,4,64]{1,0,3,2:T(4,128)} %get-tuple-element.534, f32[1,512,4,64]{1,0,3,2:T(1,128)S(1)} %copy.97, s32[]{:T(128)S(6)} %copy.116, s32[]{:T(128)} %constant.102.clone.1..sunk.1, s32[]{:T(128)} %constant.102.clone.1..sunk.1, s32[]{:T(128)} %constant.102.clone.1..sunk.1) | dynamic-update-slice | bytes 1048580 | tf_op jit(solution)/shard_map/while/body/eval_jaxpr/while/body/jit(dynamic_update_index_in_dim)/dynamic_update_slice | solution.py:69
  775.5 5.7 copy-done.1
  781.2 7.6 fusion.149
  788.8 12.8 %multiply_reduce_fusion.3 = (f32[4,512]{1,0:T(4,128)S(1)}, f32[4,512,2048]{2,1,0:T(8,128)}) fusion(f32[4,512,2048]{2,1,0:T(8,128)} %copy-done.1, f32[4,512]{1,0:T(4,128)S(1)} %dynamic-slice_bitcast_fusion.2, pred[512,2048]{1,0:T(8,128)(4,1)S(1)} %fusion.147, bf16[2048,4,64]{0,2,1:T(8,128)(2,1)} %get-tuple-element.557, ...), kind=kOutput, calls=%fused_computation.19.clone.1 | convolution fusion | flops 557840384 | bytes 35930116 | tf_op jit(solution)/shard_map/while/body/eval_jaxpr/while/body/eval_jaxpr/qhd,khd->hqk/dot_general | solution.py:83
  801.6 12.1 %multiply_convert_fusion.7 = bf16[4,512,2048]{2,1,0:T(8,128)(2,1)S(1)} fusion(f32[4,512,2048]{2,1,0:T(8,128)} %get-tuple-element.477, f32[4,512,2048]{2,1,0:T(8,128)} %copy-done.1, f32[4,512]{1,0:T(4,128)S(1)} %get-tuple-element.478, f32[4,512]{1,0:T(4,128)S(1)} %dynamic-slice_bitcast_fusion.2, pred[512,2048]{1,0:T(8,128)(4,1)S(1)} %fusion.147), kind=kLoop, calls=%fused_computation.18.clone.1 | loop fusion | flops 25165824 | bytes 43008000 | tf_op jit(solution)/shard_map/while/body/eval_jaxpr/while/body/eval_jaxpr/convert_element_type | solution.py:88
  816.3 4.7 fusion.148
  821.5 11.1 %dynamic_update_slice.31 = f32[4,512,4,64]{1,0,3,2:T(4,128)} dynamic-update-slice(f32[4,512,4,64]{1,0,3,2:T(4,128)} %get-tuple-element.534, f32[1,512,4,64]{1,0,3,2:T(1,128)S(1)} %copy.97, s32[]{:T(128)S(6)} %copy.116, s32[]{:T(128)} %constant.102.clone.1..sunk.1, s32[]{:T(128)} %constant.102.clone.1..sunk.1, s32[]{:T(128)} %constant.102.clone.1..sunk.1) | dynamic-update-slice | bytes 1048580 | tf_op jit(solution)/shard_map/while/body/eval_jaxpr/while/body/jit(dynamic_update_index_in_dim)/dynamic_update_slice | solution.py:69
  848.8 7.2 convert_bitcast_fusion
  856.0 7.2 convolution_convert_fusion
  881.1 33.1 %all-reduce.6.cloned.1.call-done = (bf16[1024,256]{1,0:T(8,128)(2,1)}, bf16[1024,256]{1,0:T(8,128)(2,1)}, bf16[1024,256]{1,0:T(8,128)(2,1)}, bf16[256,1024]{1,0:T(8,128)(2,1)}) async-done(((bf16[1024,256]{1,0:T(8,128)(2,1)}, bf16[1024,256]{1,0:T(8,128)(2,1)}, bf16[1024,256]{1,0:T(8,128)(2,1)}, bf16[256,1024]{1,0:T(8,128)(2,1)}), (bf16[1024,256]{1,0:T(8,128)(2,1)}, bf16[1024,256]{1,0:T(8,128)(2,1)}, ...) | async-done | bytes 2097168 | tf_op jit(solution)/shard_map/psum | solution.py:253
  920.7 48.6 %reduce-scatter.11.cloned.1.call-done = bf16[512,1,1024]{2,0,1:T(8,128)(2,1)} async-done(((bf16[2048,1,1024]{2,0,1:T(8,128)(2,1)}), bf16[512,1,1024]{2,0,1:T(8,128)(2,1)}) %reduce-scatter.11.cloned.1.call-update) | async-done | bytes 1048592 | tf_op jit(solution)/shard_map/reduce_scatter | solution.py:242
  972.0 42.0 %all-reduce = (f32[1024]{0:T(1024)}, f32[1024]{0:T(1024)}, f32[2]{0:T(128)}) all-reduce(f32[1024]{0:T(1024)} %get-tuple-element.261, f32[1024]{0:T(1024)} %get-tuple-element.259, f32[2]{0:T(128)} %pad_maximum_fusion.7), channel_id=1, replica_groups=mesh['dp'=2,'head'=4,'mlp'=4] {'dp','head','mlp'}, use_global_device_ids=true, to_apply=%region_16.17 | all-reduce | flops 2050 | bytes 16400 | tf_op jit(solution)/shard_map/psum | solution.py:271
  1016.5 32.9 %reduce-scatter.7.cloned.1.call-done = bf16[512,1,1024]{2,0,1:T(8,128)(2,1)} async-done(((bf16[512,4,1024]{2,0,1:T(8,128)(2,1)}), bf16[512,1,1024]{2,0,1:T(8,128)(2,1)}) %reduce-scatter.7.cloned.1.call-update) | async-done | bytes 1048592 | tf_op jit(solution)/shard_map/reduce_scatter | solution.py:188
  (239 shorter events, 182.9 us)
Async XLA Ops:
  7.2 402.2 %copy-start = (bf16[704,1024]{1,0:T(8,128)(2,1)S(1)}, bf16[704,1024]{1,0:T(8,128)(2,1)}, u32[]{:S(2)}) copy-start(bf16[704,1024]{1,0:T(8,128)(2,1)} %param.30) | copy-start | bytes 4325380
  7.2 4.9 copy-start.36
  7.2 4.9 copy-start.19
  7.2 60.4 %all-gather.5.cloned.1.call-start = ((), (), s32[]{:S(2)}) async-start(), calls=%async_computation.4 | async-start | bytes 5242880 | tf_op jit(solution)/shard_map/all_gather | solution.py:137
  12.0 229.5 %reduce-scatter.5.cloned.1.call-start = ((), (), s32[]{:S(2)}) async-start(), calls=%async_computation.5 | async-start | bytes 10485760 | tf_op jit(solution)/shard_map/reduce_scatter | solution.py:169
  19.0 58.1 %copy-start.13 = (f32[2048,32]{0,1:T(8,128)}, f32[2048,32]{0,1:T(8,128)S(1)}, u32[]{:S(2)}) copy-start(f32[2048,32]{0,1:T(8,128)S(1)} %get-tuple-element.348) | copy-start | bytes 786436
  84.2 5.0 copy-start.20
  101.2 5.0 copy-start.20
  118.2 5.0 copy-start.20
  135.2 5.0 copy-start.20
  146.7 8.3 copy-start.4
  146.7 3.7 copy-start.23
  154.9 86.6 %copy-start.2 = (bf16[512,1,1024]{2,0,1:T(8,128)(2,1)S(1)}, bf16[512,1,1024]{2,0,1:T(8,128)(2,1)}, u32[]{:S(2)}) copy-start(bf16[512,1,1024]{2,0,1:T(8,128)(2,1)} %param.18) | copy-start | bytes 3145732
  155.0 89.8 %copy-start.28 = (f32[1024]{0:T(1024)S(1)}, f32[1024]{0:T(1024)}, u32[]{:S(2)}) copy-start(f32[1024]{0:T(1024)} %param.27) | copy-start | bytes 12292
  155.0 173.5 %all-gather.7.cloned.1.call-start = ((), (), s32[]{:S(2)}) async-start(), calls=%async_computation.6 | async-start | bytes 5242880 | tf_op jit(solution)/shard_map/all_gather | solution.py:179
  244.8 265.9 %copy-start.30 = (f32[512]{0:T(512)}, f32[512]{0:T(512)S(1)}, u32[]{:S(2)}) copy-start(f32[512]{0:T(512)S(1)} %add_rsqrt_fusion) | copy-start | bytes 6148
  247.6 161.7 %all-gather.9.cloned.1.call-start = ((), (), s32[]{:S(2)}) async-start(), calls=%async_computation.8 | async-start | bytes 5242880 | tf_op jit(solution)/shard_map/all_gather | solution.py:192
  248.2 259.2 %reduce-scatter.9.cloned.1.call-start = ((), (), s32[]{:S(2)}) async-start(), calls=%async_computation.9 | async-start | bytes 5242880 | tf_op jit(solution)/shard_map/reduce_scatter | solution.py:207
  409.3 13.1 %copy-start.16 = (bf16[1024,704]{1,0:T(8,128)(2,1)S(1)}, bf16[1024,704]{1,0:T(8,128)(2,1)}, u32[]{:S(2)}) copy-start(bf16[1024,704]{1,0:T(8,128)(2,1)} %copy.68) | copy-start | bytes 4325380
  409.3 13.1 %copy-start.17 = (bf16[1024,704]{1,0:T(8,128)(2,1)S(1)}, bf16[1024,704]{1,0:T(8,128)(2,1)}, u32[]{:S(2)}) copy-start(bf16[1024,704]{1,0:T(8,128)(2,1)} %copy.69) | copy-start | bytes 4325380
  431.9 79.3 %copy-start.5 = (bf16[512,1,1024]{2,0,1:T(8,128)(2,1)S(1)}, bf16[512,1,1024]{2,0,1:T(8,128)(2,1)}, u32[]{:S(2)}) copy-start(bf16[512,1,1024]{2,0,1:T(8,128)(2,1)} %param.31) | copy-start | bytes 3145732
  431.9 136.0 %all-gather.11.cloned.1.call-start = ((), (), s32[]{:S(2)}) async-start(), calls=%async_computation.10 | async-start | bytes 5242880 | tf_op jit(solution)/shard_map/all_gather | solution.py:213
  507.4 3.9 copy-start.7
  514.6 356.7 %all-reduce.8.cloned.1.call-start = ((), (), s32[]{:S(2)}) async-start(), calls=%async_computation.13 | async-start | bytes 9175040 | tf_op jit(solution)/shard_map/psum | solution.py:263
  514.7 12.8 %copy-start.40 = (bf16[512,4,704]{0,2,1:T(8,128)(2,1)S(1)}, bf16[512,4,704]{0,2,1:T(8,128)(2,1)}, u32[]{:S(2)}) copy-start(bf16[512,4,704]{0,2,1:T(8,128)(2,1)} %get-tuple-element.321) | copy-start | bytes 8650756
  525.1 3.3 copy-start.39
  532.8 35.2 %copy-start.24 = (bf16[256,1024]{1,0:T(8,128)(2,1)S(1)}, bf16[256,1024]{1,0:T(8,128)(2,1)}, u32[]{:S(2)}) copy-start(bf16[256,1024]{1,0:T(8,128)(2,1)} %param.26) | copy-start | bytes 1572868
  532.8 381.4 %all-reduce.6.cloned.1.call-start = ((), (), s32[]{:S(2)}) async-start(), calls=%async_computation.12 | async-start | bytes 4194304 | tf_op jit(solution)/shard_map/psum | solution.py:253
  580.6 5.9 copy-start.1
  645.1 5.9 copy-start.1
  710.4 5.8 copy-start.1
  775.5 5.8 copy-start.1
  837.9 3.3 copy-start.37
  838.1 6.7 copy-start.22
  840.0 8.8 copy-start.11
  841.2 4.7 copy-start.38
  848.7 120.6 %reduce-scatter.11.cloned.1.call-start = ((), (), s32[]{:S(2)}) async-start(), calls=%async_computation.11 | async-start | bytes 5242880 | tf_op jit(solution)/shard_map/reduce_scatter | solution.py:242
  856.0 193.4 %reduce-scatter.7.cloned.1.call-start = ((), (), s32[]{:S(2)}) async-start(), calls=%async_computation.7 | async-start | bytes 5242880 | tf_op jit(solution)/shard_map/reduce_scatter | solution.py:188
  871.3 3.1 copy-start.15
  876.4 3.4 copy-start.12
  914.2 4.3 copy-start.26
  914.2 5.4 copy-start.25
  914.2 55.1 %copy-start.3 = (bf16[512,1,1024]{2,0,1:T(8,128)(2,1)S(1)}, bf16[512,1,1024]{2,0,1:T(8,128)(2,1)}, u32[]{:S(2)}) copy-start(bf16[512,1,1024]{2,0,1:T(8,128)(2,1)} %param.18) | copy-start | bytes 3145732
  914.2 55.1 %copy-start.32 = (f32[1024]{0:T(1024)S(1)}, f32[1024]{0:T(1024)}, u32[]{:S(2)}) copy-start(f32[1024]{0:T(1024)} %param.22) | copy-start | bytes 12292
  914.2 55.1 %copy-start.34 = (f32[512]{0:T(512)S(1)}, f32[512]{0:T(512)}, u32[]{:S(2)}) copy-start(f32[512]{0:T(512)} %copy-done.33) | copy-start | bytes 6148
  918.5 130.9 %copy-start.6 = (bf16[512,1,1024]{2,0,1:T(8,128)(2,1)S(1)}, bf16[512,1,1024]{2,0,1:T(8,128)(2,1)}, u32[]{:S(2)}) copy-start(bf16[512,1,1024]{2,0,1:T(8,128)(2,1)} %param.31) | copy-start | bytes 3145732
  918.5 130.9 %copy-start.29 = (f32[1024]{0:T(1024)S(1)}, f32[1024]{0:T(1024)}, u32[]{:S(2)}) copy-start(f32[1024]{0:T(1024)} %param.27) | copy-start | bytes 12292
  918.5 130.9 %copy-start.31 = (f32[512]{0:T(512)S(1)}, f32[512]{0:T(512)}, u32[]{:S(2)}) copy-start(f32[512]{0:T(512)} %copy-done.30) | copy-start | bytes 6148
  (14 other events, 18.4 us)
Sparse Core Ops, SparseCore 0:
  12.2 55.3 all-gather.4
  155.1 86.4 reduce-scatter.4
  247.7 80.7 all-gather.6
  330.0 79.2 all-gather.8
  432.0 75.2 reduce-scatter.8
  514.7 53.1 all-gather.10
  572.2 85.7 all-reduce.7
  848.8 65.3 all-reduce.5
  917.2 52.1 reduce-scatter.10
  971.6 77.7 reduce-scatter.6
where the time goes:
time: 1070 us; the launch traced here: 1060 us
  waiting for transfers between devices  503 us (47%)
  matrix products  241 us (23%)
  other arithmetic  130 us (12%)
  local copies, waits for them, and re-layouts  117 us (11%)
  blocking collectives  42 us (4%)
  between operations  14.8 us (1%)
  loops' own time  12.4 us (1%)
    reduce_scatter x1, waiting for transfers between devices, on_device(): lax.psum_scatter(jnp.einsum('lrh,hd->lrd', part, w_out, preferred_element...  86.5 us
    reduce_scatter x1, waiting for transfers between devices, on_device(): lax.psum_scatter(input_terms.astype(jnp.bfloat16), 'mlp', scatter_dimensi...  75 us
    all_gather x1, waiting for transfers between devices, on_device(): piece = lax.all_gather(mlp_input, 'mlp', axis=1, tiled=True)  75 us
    all_gather x1, waiting for transfers between devices, on_device(): piece = lax.all_gather(out_grad, 'mlp', axis=1, tiled=True)  67.6 us
    dot_general x4, matrix products, one_block(): jnp.einsum('qhd,khd->hqk', grad_block, values, preferred_element_type=jnp...  51.3 us
    reduce_scatter x1, waiting for transfers between devices, on_device(): lax.psum_scatter(jnp.einsum('lrh,dh->lrd', part, w_project, preferred_ele...  48.6 us
    all_gather x1, waiting for transfers between devices, on_device(): piece = lax.all_gather(attn_input, 'head', axis=0, tiled=True)  48.6 us
    convert_element_type x4, other arithmetic, one_block(): score_grad = (probs * (weight_grad - jnp.sum(probs * weight_grad, axis=-1...  48.5 us
  transfers between devices with their start and end apart: 10, of which 9 were waited for; matrix products, arithmetic and copies ran while one was open for 31% of the time, Pallas kernels for 0%

commit v1 on v0

--- a/solution.py
+++ b/solution.py
@@ -250,7 +250,9 @@
     input_norm_grad, attn_gain_grad = norm_back(residual, attn_scale, attn_gain, attn_normed_grad)
     input_grad = (state_grad + input_norm_grad).astype(jnp.bfloat16)
     query_wgrad, key_wgrad, value_wgrad, out_wgrad = (
-        lax.psum(proj_wgrad[:, :width].astype(jnp.bfloat16), ("dp", "mlp")).astype(jnp.float32),
+        jnp.sum(
+            lax.all_gather(proj_wgrad[:, :width].astype(jnp.bfloat16), ("dp", "mlp")), axis=0
+        ).astype(jnp.float32),
         lax.psum(proj_wgrad[:, width : 2 * width].astype(jnp.bfloat16), ("dp", "mlp")).astype(
             jnp.float32
         ),

time: 1070 us -> 1110 us (1.037)
  waiting for transfers between devices: 503 us -> 543 us
    all_gather x0 -> x1, waiting for transfers between devices: none -> 43.7 us  [on_device(): lax.all_gather(proj_wgrad[:, :width].astype(jnp.bfloat16), ('dp', 'mlp'))]
    unnamed x89 -> x87, local copies, waits for them, and re-layouts: 25.6 us -> 25.7 us
  transfers between devices with their start and end apart: 10 -> 11, of which waited for: 9 -> 10; matrix products, arithmetic and copies ran while one was open for 31% -> 30% of each run, Pallas kernels for 0% -> 0%
where the time goes in v1:
time: 1110 us
  waiting for transfers between devices  543 us (49%)
  matrix products  241 us (22%)
  other arithmetic  134 us (12%)
  local copies, waits for them, and re-layouts  117 us (11%)
  blocking collectives  42 us (4%)
  between operations  14.7 us (1%)
  loops' own time  13.3 us (1%)
    reduce_scatter x1, waiting for transfers between devices, on_device(): lax.psum_scatter(jnp.einsum('lrh,hd->lrd', part, w_out, preferred_element...  86.5 us
    reduce_scatter x1, waiting for transfers between devices, on_device(): lax.psum_scatter(input_terms.astype(jnp.bfloat16), 'mlp', scatter_dimensi...  74.9 us
    all_gather x1, waiting for transfers between devices, on_device(): piece = lax.all_gather(mlp_input, 'mlp', axis=1, tiled=True)  74.9 us
    all_gather x1, waiting for transfers between devices, on_device(): piece = lax.all_gather(out_grad, 'mlp', axis=1, tiled=True)  67.6 us
    dot_general x4, matrix products, one_block(): jnp.einsum('qhd,khd->hqk', grad_block, values, preferred_element_type=jnp...  51.3 us
    all_gather x1, waiting for transfers between devices, on_device(): piece = lax.all_gather(attn_input, 'head', axis=0, tiled=True)  48.6 us
    convert_element_type x4, other arithmetic, one_block(): score_grad = (probs * (weight_grad - jnp.sum(probs * weight_grad, axis=-1...  48.5 us
    reduce_scatter x1, waiting for transfers between devices, on_device(): lax.psum_scatter(jnp.einsum('lrh,dh->lrd', part, w_project, preferred_ele...  48.3 us
  transfers between devices with their start and end apart: 11, of which 10 were waited for; matrix products, arithmetic and copies ran while one was open for 30% of the time, Pallas kernels for 0%

profile of v1, /device:TPU:0, one launch (start us, length us, event | category | flops | bytes accessed | tf_op | source)
XLA Modules:
  0.0 1106.7 jit_solution(10051755026222934793)
XLA Ops:
  19.0 48.6 %all-gather.7.cloned.1.call-done = bf16[2048,1,1024]{2,0,1:T(8,128)(2,1)} async-done(((bf16[512,1,1024]{2,0,1:T(8,128)(2,1)}), bf16[2048,1,1024]{2,0,1:T(8,128)(2,1)}) %all-gather.7.cloned.1.call-update) | async-done | bytes 4194320 | tf_op jit(solution)/shard_map/all_gather | solution.py:137
  67.6 5.8 fusion.45
  78.5 68.2 %while.47 = (s32[]{:T(128)}, bf16[4,512,4,64]{1,3,2,0:T(8,128)(2,1)}, f32[4,4,512,1]{2,1,3,0:T(4,128)}, s32[4]{0:T(128)S(1)}, s32[2048]{0:T(1024)S(1)}, /*index=...) while((s32[]{:T(128)}, ...), condition=%wide.region_4.0_spmd, body=%wide.region_1.4_spmd.sunk | while | flops 1123023360 | bytes 65882372 | solution.py:69
  89.2 5.5 fusion.136
  106.2 5.5 fusion.136
  123.2 5.5 fusion.136
  140.2 5.5 fusion.136
  150.4 4.6 convolution_bitcast_fusion
  155.1 86.5 %reduce-scatter.5.cloned.1.call-done = f32[512,1,1024]{2,0,1:T(8,128)} async-done(((f32[2048,1,1024]{2,0,1:T(8,128)}), f32[512,1,1024]{2,0,1:T(8,128)}) %reduce-scatter.5.cloned.1.call-update) | async-done | bytes 2097168 | tf_op jit(solution)/shard_map/reduce_scatter | solution.py:169
  253.6 74.9 %all-gather.9.cloned.1.call-done = bf16[512,4,1024]{2,0,1:T(8,128)(2,1)} async-done(((bf16[512,1,1024]{2,0,1:T(8,128)(2,1)}), bf16[512,4,1024]{2,0,1:T(8,128)(2,1)}) %all-gather.9.cloned.1.call-update) | async-done | bytes 4194320 | tf_op jit(solution)/shard_map/all_gather | solution.py:179
  328.6 13.2 %fusion.74 = f32[512,4,1408]{0,2,1:T(8,128)} fusion(bf16[512,4,1024]{2,0,1:T(8,128)(2,1)} %all-gather.9.cloned.1.call-done, bf16[1024,704]{1,0:T(8,128)(2,1)} %copy.69, bf16[1024,704]{1,0:T(8,128)(2,1)} %copy.68), kind=kOutput, calls=%fused_computation.106 | convolution fusion | flops 5911347200 | bytes 18612224 | tf_op jit(solution)/shard_map/lrd,df->lrf/dot_general | solution.py:180
  341.8 67.6 %all-gather.11.cloned.1.call-done = bf16[512,4,1024]{2,0,1:T(8,128)(2,1)} async-done(((bf16[512,1,1024]{2,0,1:T(8,128)(2,1)}), bf16[512,4,1024]{2,0,1:T(8,128)(2,1)}) %all-gather.11.cloned.1.call-update) | async-done | bytes 4194320 | tf_op jit(solution)/shard_map/all_gather | solution.py:192
  409.4 10.6 multiply_convert_fusion.2
  422.5 9.4 fusion.49
  432.5 74.9 %reduce-scatter.9.cloned.1.call-done = bf16[512,1,1024]{2,0,1:T(8,128)(2,1)} async-done(((bf16[512,4,1024]{2,0,1:T(8,128)(2,1)}), bf16[512,1,1024]{2,0,1:T(8,128)(2,1)}) %reduce-scatter.9.cloned.1.call-update) | async-done | bytes 1048592 | tf_op jit(solution)/shard_map/reduce_scatter | solution.py:207
  514.7 10.4 bitcast_convert_fusion
  532.9 35.1 %all-gather.13.cloned.1.call-done = bf16[2048,1,1024]{2,0,1:T(8,128)(2,1)} async-done(((bf16[512,1,1024]{2,0,1:T(8,128)(2,1)}), bf16[2048,1,1024]{2,0,1:T(8,128)(2,1)}) %all-gather.13.cloned.1.call-update) | async-done | bytes 4194320 | tf_op jit(solution)/shard_map/all_gather | solution.py:213
  572.5 261.2 %while.48 = (s32[]{:T(128)}, f32[2048,4,64]{0,2,1:T(8,128)}, f32[2048,4,64]{0,2,1:T(8,128)}, f32[4,512,4,64]{1,0,3,2:T(4,128)}, s32[4]{0:T(128)S(1)}, /*index=5*...) while((s32[]{:T(128)}, f32[2048,4,64]{0,2,1:T(8,128)}, ...), condition=%wide.region_12.13_spmd.clone, body=%wide.region_10.12_spmd.clone.sunk | while | flops 2753165824 | bytes 212412720 | solution.py:105
  580.9 5.8 copy-done.1
  586.7 7.2 fusion.149
  593.9 13.0 %multiply_reduce_fusion.3 = (f32[4,512]{1,0:T(4,128)S(1)}, f32[4,512,2048]{2,1,0:T(8,128)}) fusion(f32[4,512,2048]{2,1,0:T(8,128)} %copy-done.1, f32[4,512]{1,0:T(4,128)S(1)} %dynamic-slice_bitcast_fusion.2, pred[512,2048]{1,0:T(8,128)(4,1)S(1)} %fusion.147, bf16[2048,4,64]{0,2,1:T(8,128)(2,1)} %get-tuple-element.556, ...), kind=kOutput, calls=%fused_computation.19.clone.1 | convolution fusion | flops 557840384 | bytes 35930116 | tf_op jit(solution)/shard_map/while/body/eval_jaxpr/while/body/eval_jaxpr/qhd,khd->hqk/dot_general | solution.py:83
  606.8 12.3 %multiply_convert_fusion.7 = bf16[4,512,2048]{2,1,0:T(8,128)(2,1)S(1)} fusion(f32[4,512,2048]{2,1,0:T(8,128)} %get-tuple-element.476, f32[4,512,2048]{2,1,0:T(8,128)} %copy-done.1, f32[4,512]{1,0:T(4,128)S(1)} %get-tuple-element.477, f32[4,512]{1,0:T(4,128)S(1)} %dynamic-slice_bitcast_fusion.2, pred[512,2048]{1,0:T(8,128)(4,1)S(1)} %fusion.147), kind=kLoop, calls=%fused_computation.18.clone.1 | loop fusion | flops 25165824 | bytes 43008000 | tf_op jit(solution)/shard_map/while/body/eval_jaxpr/while/body/eval_jaxpr/convert_element_type | solution.py:88
  626.3 11.1 %dynamic_update_slice.31 = f32[4,512,4,64]{1,0,3,2:T(4,128)} dynamic-update-slice(f32[4,512,4,64]{1,0,3,2:T(4,128)} %get-tuple-element.533, f32[1,512,4,64]{1,0,3,2:T(1,128)S(1)} %copy.97, s32[]{:T(128)S(6)} %copy.116, s32[]{:T(128)} %constant.103.clone.1..sunk.1, s32[]{:T(128)} %constant.103.clone.1..sunk.1, s32[]{:T(128)} %constant.103.clone.1..sunk.1) | dynamic-update-slice | bytes 1048580 | tf_op jit(solution)/shard_map/while/body/eval_jaxpr/while/body/jit(dynamic_update_index_in_dim)/dynamic_update_slice | solution.py:69
  645.6 5.9 copy-done.1
  651.5 7.6 fusion.149
  659.1 12.8 %multiply_reduce_fusion.3 = (f32[4,512]{1,0:T(4,128)S(1)}, f32[4,512,2048]{2,1,0:T(8,128)}) fusion(f32[4,512,2048]{2,1,0:T(8,128)} %copy-done.1, f32[4,512]{1,0:T(4,128)S(1)} %dynamic-slice_bitcast_fusion.2, pred[512,2048]{1,0:T(8,128)(4,1)S(1)} %fusion.147, bf16[2048,4,64]{0,2,1:T(8,128)(2,1)} %get-tuple-element.556, ...), kind=kOutput, calls=%fused_computation.19.clone.1 | convolution fusion | flops 557840384 | bytes 35930116 | tf_op jit(solution)/shard_map/while/body/eval_jaxpr/while/body/eval_jaxpr/qhd,khd->hqk/dot_general | solution.py:83
  671.8 12.1 %multiply_convert_fusion.7 = bf16[4,512,2048]{2,1,0:T(8,128)(2,1)S(1)} fusion(f32[4,512,2048]{2,1,0:T(8,128)} %get-tuple-element.476, f32[4,512,2048]{2,1,0:T(8,128)} %copy-done.1, f32[4,512]{1,0:T(4,128)S(1)} %get-tuple-element.477, f32[4,512]{1,0:T(4,128)S(1)} %dynamic-slice_bitcast_fusion.2, pred[512,2048]{1,0:T(8,128)(4,1)S(1)} %fusion.147), kind=kLoop, calls=%fused_computation.18.clone.1 | loop fusion | flops 25165824 | bytes 43008000 | tf_op jit(solution)/shard_map/while/body/eval_jaxpr/while/body/eval_jaxpr/convert_element_type | solution.py:88
  686.6 4.7 fusion.148
  691.8 11.1 %dynamic_update_slice.31 = f32[4,512,4,64]{1,0,3,2:T(4,128)} dynamic-update-slice(f32[4,512,4,64]{1,0,3,2:T(4,128)} %get-tuple-element.533, f32[1,512,4,64]{1,0,3,2:T(1,128)S(1)} %copy.97, s32[]{:T(128)S(6)} %copy.116, s32[]{:T(128)} %constant.103.clone.1..sunk.1, s32[]{:T(128)} %constant.103.clone.1..sunk.1, s32[]{:T(128)} %constant.103.clone.1..sunk.1) | dynamic-update-slice | bytes 1048580 | tf_op jit(solution)/shard_map/while/body/eval_jaxpr/while/body/jit(dynamic_update_index_in_dim)/dynamic_update_slice | solution.py:69
  711.0 5.7 copy-done.1
  716.8 7.6 fusion.149
  724.3 12.8 %multiply_reduce_fusion.3 = (f32[4,512]{1,0:T(4,128)S(1)}, f32[4,512,2048]{2,1,0:T(8,128)}) fusion(f32[4,512,2048]{2,1,0:T(8,128)} %copy-done.1, f32[4,512]{1,0:T(4,128)S(1)} %dynamic-slice_bitcast_fusion.2, pred[512,2048]{1,0:T(8,128)(4,1)S(1)} %fusion.147, bf16[2048,4,64]{0,2,1:T(8,128)(2,1)} %get-tuple-element.556, ...), kind=kOutput, calls=%fused_computation.19.clone.1 | convolution fusion | flops 557840384 | bytes 35930116 | tf_op jit(solution)/shard_map/while/body/eval_jaxpr/while/body/eval_jaxpr/qhd,khd->hqk/dot_general | solution.py:83
  737.1 12.1 %multiply_convert_fusion.7 = bf16[4,512,2048]{2,1,0:T(8,128)(2,1)S(1)} fusion(f32[4,512,2048]{2,1,0:T(8,128)} %get-tuple-element.476, f32[4,512,2048]{2,1,0:T(8,128)} %copy-done.1, f32[4,512]{1,0:T(4,128)S(1)} %get-tuple-element.477, f32[4,512]{1,0:T(4,128)S(1)} %dynamic-slice_bitcast_fusion.2, pred[512,2048]{1,0:T(8,128)(4,1)S(1)} %fusion.147), kind=kLoop, calls=%fused_computation.18.clone.1 | loop fusion | flops 25165824 | bytes 43008000 | tf_op jit(solution)/shard_map/while/body/eval_jaxpr/while/body/eval_jaxpr/convert_element_type | solution.py:88
  751.8 4.7 fusion.148
  757.1 11.1 %dynamic_update_slice.31 = f32[4,512,4,64]{1,0,3,2:T(4,128)} dynamic-update-slice(f32[4,512,4,64]{1,0,3,2:T(4,128)} %get-tuple-element.533, f32[1,512,4,64]{1,0,3,2:T(1,128)S(1)} %copy.97, s32[]{:T(128)S(6)} %copy.116, s32[]{:T(128)} %constant.103.clone.1..sunk.1, s32[]{:T(128)} %constant.103.clone.1..sunk.1, s32[]{:T(128)} %constant.103.clone.1..sunk.1) | dynamic-update-slice | bytes 1048580 | tf_op jit(solution)/shard_map/while/body/eval_jaxpr/while/body/jit(dynamic_update_index_in_dim)/dynamic_update_slice | solution.py:69
  776.3 5.7 copy-done.1
  782.1 7.5 fusion.149
  789.6 12.8 %multiply_reduce_fusion.3 = (f32[4,512]{1,0:T(4,128)S(1)}, f32[4,512,2048]{2,1,0:T(8,128)}) fusion(f32[4,512,2048]{2,1,0:T(8,128)} %copy-done.1, f32[4,512]{1,0:T(4,128)S(1)} %dynamic-slice_bitcast_fusion.2, pred[512,2048]{1,0:T(8,128)(4,1)S(1)} %fusion.147, bf16[2048,4,64]{0,2,1:T(8,128)(2,1)} %get-tuple-element.556, ...), kind=kOutput, calls=%fused_computation.19.clone.1 | convolution fusion | flops 557840384 | bytes 35930116 | tf_op jit(solution)/shard_map/while/body/eval_jaxpr/while/body/eval_jaxpr/qhd,khd->hqk/dot_general | solution.py:83
  802.4 12.1 %multiply_convert_fusion.7 = bf16[4,512,2048]{2,1,0:T(8,128)(2,1)S(1)} fusion(f32[4,512,2048]{2,1,0:T(8,128)} %get-tuple-element.476, f32[4,512,2048]{2,1,0:T(8,128)} %copy-done.1, f32[4,512]{1,0:T(4,128)S(1)} %get-tuple-element.477, f32[4,512]{1,0:T(4,128)S(1)} %dynamic-slice_bitcast_fusion.2, pred[512,2048]{1,0:T(8,128)(4,1)S(1)} %fusion.147), kind=kLoop, calls=%fused_computation.18.clone.1 | loop fusion | flops 25165824 | bytes 43008000 | tf_op jit(solution)/shard_map/while/body/eval_jaxpr/while/body/eval_jaxpr/convert_element_type | solution.py:88
  817.1 4.7 fusion.148
  822.3 11.1 %dynamic_update_slice.31 = f32[4,512,4,64]{1,0,3,2:T(4,128)} dynamic-update-slice(f32[4,512,4,64]{1,0,3,2:T(4,128)} %get-tuple-element.533, f32[1,512,4,64]{1,0,3,2:T(1,128)S(1)} %copy.97, s32[]{:T(128)S(6)} %copy.116, s32[]{:T(128)} %constant.103.clone.1..sunk.1, s32[]{:T(128)} %constant.103.clone.1..sunk.1, s32[]{:T(128)} %constant.103.clone.1..sunk.1) | dynamic-update-slice | bytes 1048580 | tf_op jit(solution)/shard_map/while/body/eval_jaxpr/while/body/jit(dynamic_update_index_in_dim)/dynamic_update_slice | solution.py:69
  850.3 7.3 convert_bitcast_fusion
  857.6 7.1 convolution_convert_fusion
  882.5 29.2 %all-reduce.6.cloned.1.call-done = (bf16[1024,256]{1,0:T(8,128)(2,1)}, bf16[1024,256]{1,0:T(8,128)(2,1)}, bf16[256,1024]{1,0:T(8,128)(2,1)}) async-done(((bf16[1024,256]{1,0:T(8,128)(2,1)}, bf16[1024,256]{1,0:T(8,128)(2,1)}, bf16[256,1024]{1,0:T(8,128)(2,1)}), (bf16[1024,256]{1,0:T(8,128)(2,1)}, bf16[1024,256]{1,0:T(8,128)(2,1)}, bf16[256,1024]{1,0:T(8,128)(2,1)})) %all-reduce.6.cloned.1.call-update) | async-done | bytes 1572880 | tf_op jit(solution)/shard_map/psum | solution.py:256
  917.0 43.7 %all-gather.15.cloned.1.call-done = bf16[8192,256]{1,0:T(8,128)(2,1)} async-done(((bf16[1024,256]{1,0:T(8,128)(2,1)}), bf16[8192,256]{1,0:T(8,128)(2,1)}) %all-gather.15.cloned.1.call-update) | async-done | bytes 4194320 | tf_op jit(solution)/shard_map/all_gather | solution.py:254
  966.7 48.3 %reduce-scatter.11.cloned.1.call-done = bf16[512,1,1024]{2,0,1:T(8,128)(2,1)} async-done(((bf16[2048,1,1024]{2,0,1:T(8,128)(2,1)}), bf16[512,1,1024]{2,0,1:T(8,128)(2,1)}) %reduce-scatter.11.cloned.1.call-update) | async-done | bytes 1048592 | tf_op jit(solution)/shard_map/reduce_scatter | solution.py:242
  1017.7 42.0 %all-reduce = (f32[1024]{0:T(1024)}, f32[1024]{0:T(1024)}, f32[2]{0:T(128)}) all-reduce(f32[1024]{0:T(1024)} %get-tuple-element.261, f32[1024]{0:T(1024)} %get-tuple-element.259, f32[2]{0:T(128)} %pad_maximum_fusion.7), channel_id=1, replica_groups=mesh['dp'=2,'head'=4,'mlp'=4] {'dp','head','mlp'}, use_global_device_ids=true, to_apply=%region_16.17 | all-reduce | flops 2050 | bytes 16400 | tf_op jit(solution)/shard_map/psum | solution.py:273
  1062.2 33.1 %reduce-scatter.7.cloned.1.call-done = bf16[512,1,1024]{2,0,1:T(8,128)(2,1)} async-done(((bf16[512,4,1024]{2,0,1:T(8,128)(2,1)}), bf16[512,1,1024]{2,0,1:T(8,128)(2,1)}) %reduce-scatter.7.cloned.1.call-update) | async-done | bytes 1048592 | tf_op jit(solution)/shard_map/reduce_scatter | solution.py:188
  (241 shorter events, 193.1 us)
Async XLA Ops:
  7.2 402.2 %copy-start = (bf16[704,1024]{1,0:T(8,128)(2,1)S(1)}, bf16[704,1024]{1,0:T(8,128)(2,1)}, u32[]{:S(2)}) copy-start(bf16[704,1024]{1,0:T(8,128)(2,1)} %param.30) | copy-start | bytes 4325380
  7.2 4.9 copy-start.35
  7.2 4.9 copy-start.19
  7.2 60.4 %all-gather.7.cloned.1.call-start = ((), (), s32[]{:S(2)}) async-start(), calls=%async_computation.4 | async-start | bytes 5242880 | tf_op jit(solution)/shard_map/all_gather | solution.py:137
  12.0 229.5 %reduce-scatter.5.cloned.1.call-start = ((), (), s32[]{:S(2)}) async-start(), calls=%async_computation.5 | async-start | bytes 10485760 | tf_op jit(solution)/shard_map/reduce_scatter | solution.py:169
  19.0 58.1 %copy-start.13 = (f32[2048,32]{0,1:T(8,128)}, f32[2048,32]{0,1:T(8,128)S(1)}, u32[]{:S(2)}) copy-start(f32[2048,32]{0,1:T(8,128)S(1)} %get-tuple-element.347) | copy-start | bytes 786436
  84.2 5.0 copy-start.20
  101.3 5.0 copy-start.20
  118.3 5.0 copy-start.20
  135.3 5.0 copy-start.20
  146.7 8.3 copy-start.4
  146.7 3.7 copy-start.23
  155.0 86.6 %copy-start.2 = (bf16[512,1,1024]{2,0,1:T(8,128)(2,1)S(1)}, bf16[512,1,1024]{2,0,1:T(8,128)(2,1)}, u32[]{:S(2)}) copy-start(bf16[512,1,1024]{2,0,1:T(8,128)(2,1)} %param.18) | copy-start | bytes 3145732
  155.0 89.8 %copy-start.27 = (f32[1024]{0:T(1024)S(1)}, f32[1024]{0:T(1024)}, u32[]{:S(2)}) copy-start(f32[1024]{0:T(1024)} %param.27) | copy-start | bytes 12292
  155.0 173.5 %all-gather.9.cloned.1.call-start = ((), (), s32[]{:S(2)}) async-start(), calls=%async_computation.6 | async-start | bytes 5242880 | tf_op jit(solution)/shard_map/all_gather | solution.py:179
  244.8 265.9 %copy-start.29 = (f32[512]{0:T(512)}, f32[512]{0:T(512)S(1)}, u32[]{:S(2)}) copy-start(f32[512]{0:T(512)S(1)} %add_rsqrt_fusion) | copy-start | bytes 6148
  247.6 161.7 %all-gather.11.cloned.1.call-start = ((), (), s32[]{:S(2)}) async-start(), calls=%async_computation.8 | async-start | bytes 5242880 | tf_op jit(solution)/shard_map/all_gather | solution.py:192
  248.2 259.2 %reduce-scatter.9.cloned.1.call-start = ((), (), s32[]{:S(2)}) async-start(), calls=%async_computation.9 | async-start | bytes 5242880 | tf_op jit(solution)/shard_map/reduce_scatter | solution.py:207
  409.4 13.1 %copy-start.16 = (bf16[1024,704]{1,0:T(8,128)(2,1)S(1)}, bf16[1024,704]{1,0:T(8,128)(2,1)}, u32[]{:S(2)}) copy-start(bf16[1024,704]{1,0:T(8,128)(2,1)} %copy.68) | copy-start | bytes 4325380
  409.4 13.1 %copy-start.17 = (bf16[1024,704]{1,0:T(8,128)(2,1)S(1)}, bf16[1024,704]{1,0:T(8,128)(2,1)}, u32[]{:S(2)}) copy-start(bf16[1024,704]{1,0:T(8,128)(2,1)} %copy.69) | copy-start | bytes 4325380
  431.9 79.3 %copy-start.5 = (bf16[512,1,1024]{2,0,1:T(8,128)(2,1)S(1)}, bf16[512,1,1024]{2,0,1:T(8,128)(2,1)}, u32[]{:S(2)}) copy-start(bf16[512,1,1024]{2,0,1:T(8,128)(2,1)} %param.31) | copy-start | bytes 3145732
  432.0 136.0 %all-gather.13.cloned.1.call-start = ((), (), s32[]{:S(2)}) async-start(), calls=%async_computation.10 | async-start | bytes 5242880 | tf_op jit(solution)/shard_map/all_gather | solution.py:213
  507.4 3.8 copy-start.7
  514.6 358.1 %all-reduce.8.cloned.1.call-start = ((), (), s32[]{:S(2)}) async-start(), calls=%async_computation.14 | async-start | bytes 9175040 | tf_op jit(solution)/shard_map/psum | solution.py:265
  514.7 12.8 %copy-start.39 = (bf16[512,4,704]{0,2,1:T(8,128)(2,1)S(1)}, bf16[512,4,704]{0,2,1:T(8,128)(2,1)}, u32[]{:S(2)}) copy-start(bf16[512,4,704]{0,2,1:T(8,128)(2,1)} %get-tuple-element.320) | copy-start | bytes 8650756
  525.2 3.3 copy-start.38
  532.8 35.2 %copy-start.24 = (bf16[256,1024]{1,0:T(8,128)(2,1)S(1)}, bf16[256,1024]{1,0:T(8,128)(2,1)}, u32[]{:S(2)}) copy-start(bf16[256,1024]{1,0:T(8,128)(2,1)} %param.26) | copy-start | bytes 1572868
  532.8 378.9 %all-reduce.6.cloned.1.call-start = ((), (), s32[]{:S(2)}) async-start(), calls=%async_computation.13 | async-start | bytes 3145728 | tf_op jit(solution)/shard_map/psum | solution.py:256
  580.9 5.9 copy-start.1
  645.6 5.9 copy-start.1
  711.0 5.8 copy-start.1
  776.3 5.8 copy-start.1
  838.8 3.3 copy-start.36
  838.9 6.7 copy-start.22
  840.8 9.5 copy-start.11
  842.1 4.7 copy-start.37
  849.5 111.3 %all-gather.15.cloned.1.call-start = ((), (), s32[]{:S(2)}) async-start(), calls=%async_computation.12 | async-start | bytes 4718592 | tf_op jit(solution)/shard_map/all_gather | solution.py:254
  850.3 164.8 %reduce-scatter.11.cloned.1.call-start = ((), (), s32[]{:S(2)}) async-start(), calls=%async_computation.11 | async-start | bytes 5242880 | tf_op jit(solution)/shard_map/reduce_scatter | solution.py:242
  857.6 237.7 %reduce-scatter.7.cloned.1.call-start = ((), (), s32[]{:S(2)}) async-start(), calls=%async_computation.7 | async-start | bytes 5242880 | tf_op jit(solution)/shard_map/reduce_scatter | solution.py:188
  872.8 3.1 copy-start.15
  877.8 3.4 copy-start.12
  911.7 4.2 copy-start.25
  960.8 54.3 %copy-start.3 = (bf16[512,1,1024]{2,0,1:T(8,128)(2,1)S(1)}, bf16[512,1,1024]{2,0,1:T(8,128)(2,1)}, u32[]{:S(2)}) copy-start(bf16[512,1,1024]{2,0,1:T(8,128)(2,1)} %param.18) | copy-start | bytes 3145732
  960.8 54.3 %copy-start.31 = (f32[1024]{0:T(1024)S(1)}, f32[1024]{0:T(1024)}, u32[]{:S(2)}) copy-start(f32[1024]{0:T(1024)} %param.22) | copy-start | bytes 12292
  960.8 54.3 %copy-start.33 = (f32[512]{0:T(512)S(1)}, f32[512]{0:T(512)}, u32[]{:S(2)}) copy-start(f32[512]{0:T(512)} %copy-done.32) | copy-start | bytes 6148
  964.6 130.7 %copy-start.6 = (bf16[512,1,1024]{2,0,1:T(8,128)(2,1)S(1)}, bf16[512,1,1024]{2,0,1:T(8,128)(2,1)}, u32[]{:S(2)}) copy-start(bf16[512,1,1024]{2,0,1:T(8,128)(2,1)} %param.31) | copy-start | bytes 3145732
  964.6 130.7 %copy-start.28 = (f32[1024]{0:T(1024)S(1)}, f32[1024]{0:T(1024)}, u32[]{:S(2)}) copy-start(f32[1024]{0:T(1024)} %param.27) | copy-start | bytes 12292
  964.6 130.7 %copy-start.30 = (f32[512]{0:T(512)S(1)}, f32[512]{0:T(512)}, u32[]{:S(2)}) copy-start(f32[512]{0:T(512)} %copy-done.29) | copy-start | bytes 6148
  (14 other events, 18.3 us)
Sparse Core Ops, SparseCore 0:
  12.2 55.3 all-gather.6
  155.1 86.4 reduce-scatter.4
  247.8 80.7 all-gather.8
  330.1 79.2 all-gather.10
  432.1 75.2 reduce-scatter.8
  514.8 53.1 all-gather.12
  572.2 85.7 all-reduce.7
  849.6 62.0 all-reduce.5
  913.9 46.8 all-gather.14
  963.6 51.4 reduce-scatter.10
  1017.5 77.7 reduce-scatter.6
